TPU v7x, 128 devices: a whole 4x4x4 slice. The times are simulated.
128 devices in a mesh: loop: 8 (over x_lo, z), group: 16 (over y, x_hi, core).
Axes of the slice: x: 4 (x_hi: 2, x_lo: 2; x = x_hi * 2 + x_lo), y: 4, z: 4, core: 2. Of those that a mesh axis runs over, the one named last changes fastest.
Arguments:
- images: bfloat16 [16384, 1152], P(('loop', 'group')), may hold values from -1 to 1, as said below
- texts: bfloat16 [16384, 1152], P(('loop', 'group')), may hold values from -1 to 1, as said below
- logit_scale: float32 [1], replicated, may hold values from 8 to 14
- bias: float32 [1], replicated, may hold values from -6 to -3
Outputs:
- grad_images: float32 [16384, 1152], P(('loop', 'group'))
- grad_texts: float32 [16384, 1152], P(('loop', 'group'))
Inputs may be any that keep to these rules, and one draw needn't show every extreme that they name: `images`: real-valued embeddings. `texts`: real-valued embeddings.
All inputs are finite; a program needn't handle non-finite values.
Results may differ from a plain program's by a relative error of at most 0.012.
Values may be sent and summed in bfloat16 or wider, within the bound.
A program may use at most 128 MiB of HBM per device.

v0:
```python
import jax
import jax.numpy as jnp
from jax import lax
from jax.sharding import PartitionSpec as P

STEPS = 4


def from_behind(block, axis, distance):
    devices = range(lax.axis_size(axis))
    route = [((i - distance) % len(devices), i) for i in devices]
    return lax.ppermute(block, axis, route)


def normalize(values):
    wide = values.astype(jnp.float32)
    norms = jnp.sqrt(jnp.sum(wide * wide, axis=-1, keepdims=True) + 1e-06)
    return (wide / norms, norms)


def unnormalize(normed, norms, upstream):
    inner = jnp.sum(normed * upstream, axis=-1, keepdims=True)
    return (upstream - normed * inner) / norms


def pool_rows(rows):
    return lax.all_gather(rows, "group", axis=0, tiled=True)


def local(images, texts, logit_scale, bias):
    tok_rows = images.shape[0]
    loops = lax.axis_size("loop")
    inormed, inorm = normalize(images)
    tnormed, tnorm = normalize(texts)
    ibf = inormed.astype(jnp.bfloat16)
    tbf = tnormed.astype(jnp.bfloat16)
    scale = logit_scale[0]
    shift = bias[0]
    group_at = lax.axis_index("group")
    visiting = tbf
    visiting = pool_rows(visiting)
    dimage = jnp.zeros(ibf.shape, jnp.float32)
    carried = jnp.zeros(texts.shape, jnp.float32)
    for step in range(STEPS):
        if step > 0:
            visiting = from_behind(visiting, "loop", 1)
        logits = scale * jnp.dot(ibf, visiting.T, preferred_element_type=jnp.float32) + shift
        if step == 0:
            row_ids = lax.broadcasted_iota(jnp.int32, logits.shape, 0)
            col_ids = lax.broadcasted_iota(jnp.int32, logits.shape, 1)
            positive = col_ids == group_at * tok_rows + row_ids
            signs = jnp.where(positive, 1.0, -1.0).astype(jnp.float32)
            slopes = (-signs * jax.nn.sigmoid(-signs * logits)).astype(jnp.bfloat16)
        else:
            slopes = jax.nn.sigmoid(logits).astype(jnp.bfloat16)
        dimage = dimage + scale * jnp.dot(slopes, visiting, preferred_element_type=jnp.float32)
        term = scale * jnp.dot(slopes.T, ibf, preferred_element_type=jnp.float32)
        carried = carried + lax.psum_scatter(
            term.astype(jnp.bfloat16), "group", scatter_dimension=0, tiled=True
        ).astype(jnp.float32)
        if step < STEPS - 1:
            carried = from_behind(carried, "loop", 1)
    carried = from_behind(carried, "loop", (1 - STEPS) % loops)
    return (unnormalize(inormed, inorm, dimage), unnormalize(tnormed, tnorm, carried))


def solution(mesh):
    in_specs = (P(("loop", "group"), None), P(("loop", "group"), None), P(), P())
    out_specs = (P(("loop", "group"), None), P(("loop", "group"), None))
    return jax.shard_map(local, mesh=mesh, in_specs=in_specs, out_specs=out_specs, check_vma=False)
```

profile of v0, /device:TPU:32, one launch (start us, length us, event | category | flops | bytes accessed | tf_op | source)
XLA Modules:
  0.0 570.9 jit_solution(7185998922708276538)
XLA Ops:
  7.2 0.0 all-gather.2.cloned.1.call-start
  7.2 1.1 fusion.32
  8.3 1.8 fusion.34
  10.1 0.0 all-gather.2.cloned.1.call-update
  10.2 0.0 reduce-scatter.5.cloned.1.call-start
  11.5 1.1 fusion.31
  12.6 57.7 %all-gather.2.cloned.1.call-done = bf16[2048,1152]{1,0:T(8,128)(2,1)} async-done(((bf16[128,1152]{1,0:T(8,128)(2,1)}), bf16[2048,1152]{1,0:T(8,128)(2,1)}) %all-gather.2.cloned.1.call-update) | async-done | bytes 4718608 | tf_op jit(solution)/shard_map/all_gather | solution.py:27
  70.3 0.0 copy-start
  70.3 4.2 fusion.27
  74.6 0.0 copy-done
  74.6 3.6 fusion
  78.2 0.0 reduce-scatter.5.cloned.1.call-update
  78.2 0.0 reduce-scatter.7.cloned.1.call-start
  78.3 1.6 collective-permute-start
  79.9 102.6 %collective-permute-done = bf16[2048,1152]{1,0:T(8,128)(2,1)S(1)} collective-permute-done((bf16[2048,1152]{1,0:T(8,128)(2,1)}, bf16[2048,1152]{1,0:T(8,128)(2,1)S(1)}, u32[]{:S(2)}, u32[]{:S(2)}) %collective-permute-start) | collective-permute-done | bytes 4718624 | tf_op jit(solution)/shard_map/ppermute | solution.py:12
  182.5 0.0 copy-start.1
  182.6 1.7 fusion.30
  184.3 0.4 copy-done.1
  184.7 3.7 fusion.1
  188.4 0.0 reduce-scatter.7.cloned.1.call-update
  188.4 0.0 reduce-scatter.9.cloned.1.call-start
  188.4 1.6 collective-permute-start.1
  190.1 118.4 %collective-permute-done.1 = bf16[2048,1152]{1,0:T(8,128)(2,1)S(1)} collective-permute-done((bf16[2048,1152]{1,0:T(8,128)(2,1)}, bf16[2048,1152]{1,0:T(8,128)(2,1)S(1)}, u32[]{:S(2)}, u32[]{:S(2)}) %collective-permute-start.1) | collective-permute-done | bytes 4718624 | tf_op jit(solution)/shard_map/ppermute | solution.py:12
  308.5 0.0 copy-start.2
  308.5 1.7 fusion.29
  310.2 0.4 copy-done.2
  310.6 3.7 fusion.2
  314.3 0.0 reduce-scatter.9.cloned.1.call-update
  314.4 0.0 reduce-scatter.11.cloned.1.call-start
  314.4 0.1 collective-permute-start.2
  314.5 120.3 %collective-permute-done.2 = bf16[2048,1152]{1,0:T(8,128)(2,1)S(1)} collective-permute-done((bf16[2048,1152]{1,0:T(8,128)(2,1)}, bf16[2048,1152]{1,0:T(8,128)(2,1)S(1)}, u32[]{:S(2)}, u32[]{:S(2)}) %collective-permute-start.2) | collective-permute-done | bytes 4718624 | tf_op jit(solution)/shard_map/ppermute | solution.py:12
  434.8 0.0 copy-start.4
  434.8 1.7 fusion.28
  436.5 0.5 copy-done.4
  437.1 3.6 fusion.3
  440.7 0.0 reduce-scatter.11.cloned.1.call-update
  440.8 0.0 reduce-scatter.5.cloned.1.call-done
  440.8 1.0 convert_element_type.57
  441.8 0.3 collective-permute-start.3
  442.1 30.8 %collective-permute-done.3 = f32[128,1152]{1,0:T(8,128)} collective-permute-done((f32[128,1152]{1,0:T(8,128)S(1)}, f32[128,1152]{1,0:T(8,128)}, u32[]{:S(2)}, u32[]{:S(2)}) %collective-permute-start.3) | collective-permute-done | bytes 589856 | tf_op jit(solution)/shard_map/ppermute | solution.py:12
  472.9 0.0 reduce-scatter.7.cloned.1.call-done
  472.9 1.2 convert_add_fusion.2
  474.1 0.1 collective-permute-start.4
  474.2 3.5 fusion.43
  477.7 10.6 %collective-permute-done.4 = f32[128,1152]{1,0:T(8,128)} collective-permute-done((f32[128,1152]{1,0:T(8,128)S(1)}, f32[128,1152]{1,0:T(8,128)}, u32[]{:S(2)}, u32[]{:S(2)}) %collective-permute-start.4) | collective-permute-done | bytes 589856 | tf_op jit(solution)/shard_map/ppermute | solution.py:12
  488.3 0.0 reduce-scatter.9.cloned.1.call-done
  488.3 1.2 convert_add_fusion.1
  489.5 0.1 collective-permute-start.5
  489.6 3.8 convolution_add_fusion.2
  493.4 3.2 convolution_add_fusion.1
  496.7 6.2 %collective-permute-done.5 = f32[128,1152]{1,0:T(8,128)} collective-permute-done((f32[128,1152]{1,0:T(8,128)S(1)}, f32[128,1152]{1,0:T(8,128)}, u32[]{:S(2)}, u32[]{:S(2)}) %collective-permute-start.5) | collective-permute-done | bytes 589856 | tf_op jit(solution)/shard_map/ppermute | solution.py:12
  502.8 44.3 %reduce-scatter.11.cloned.1.call-done = bf16[128,1152]{1,0:T(8,128)(2,1)} async-done(((bf16[2048,1152]{1,0:T(8,128)(2,1)}), bf16[128,1152]{1,0:T(8,128)(2,1)}) %reduce-scatter.11.cloned.1.call-update) | async-done | bytes 294928 | tf_op jit(solution)/shard_map/reduce_scatter | solution.py:58
  547.1 1.2 convert_add_fusion
  548.3 0.0 copy-start.3
  548.4 1.6 collective-permute-start.6
  550.0 3.3 multiply_reduce_fusion.1
  553.3 1.0 subtract_divide_fusion.1
  554.3 8.9 %collective-permute-done.6 = f32[128,1152]{1,0:T(8,128)S(1)} collective-permute-done((f32[128,1152]{1,0:T(8,128)S(1)}, f32[128,1152]{1,0:T(8,128)S(1)}, u32[]{:S(2)}, u32[]{:S(2)}) %collective-permute-start.6) | collective-permute-done | bytes 589856 | tf_op jit(solution)/shard_map/ppermute | solution.py:12
  563.2 0.0 copy-done.3
  563.2 0.2 multiply_reduce_fusion
  563.4 1.0 subtract_divide_fusion
  (3 shorter events, 0.0 us)
Async XLA Ops:
  7.2 63.2 %all-gather.2.cloned.1.call-start = ((), (), s32[]{:S(2)}) async-start(), calls=%async_computation.4 | async-start | bytes 5013504 | tf_op jit(solution)/shard_map/all_gather | solution.py:27
  10.2 430.6 %reduce-scatter.5.cloned.1.call-start = ((), (), s32[]{:S(2)}) async-start(), calls=%async_computation.5 | async-start | bytes 5013504 | tf_op jit(solution)/shard_map/reduce_scatter | solution.py:58
  70.3 4.2 copy-start
  78.2 394.7 %reduce-scatter.7.cloned.1.call-start = ((), (), s32[]{:S(2)}) async-start(), calls=%async_computation.6 | async-start | bytes 5013504 | tf_op jit(solution)/shard_map/reduce_scatter | solution.py:58
  78.3 104.3 %collective-permute-start = (bf16[2048,1152]{1,0:T(8,128)(2,1)}, bf16[2048,1152]{1,0:T(8,128)(2,1)S(1)}, u32[]{:S(2)}, u32[]{:S(2)}) collective-permute-start(bf16[2048,1152]{1,0:T(8,128)(2,1)} %all-gather.2.cloned.1.call-done), channel_id=1, source_target_pairs={{112,0},{0,16},{16,32},{32,48},{48,64},{64,80},{80,96},{96,112},{1... | collective-permute-start | bytes 14155784 | tf_op jit(solution)/shard_map/ppermute | solution.py:12
  182.5 2.1 copy-start.1
  188.4 300.0 %reduce-scatter.9.cloned.1.call-start = ((), (), s32[]{:S(2)}) async-start(), calls=%async_computation.7 | async-start | bytes 5013504 | tf_op jit(solution)/shard_map/reduce_scatter | solution.py:58
  188.4 120.1 %collective-permute-start.1 = (bf16[2048,1152]{1,0:T(8,128)(2,1)}, bf16[2048,1152]{1,0:T(8,128)(2,1)S(1)}, u32[]{:S(2)}, u32[]{:S(2)}) collective-permute-start(bf16[2048,1152]{1,0:T(8,128)(2,1)} %copy-done.1), channel_id=1, source_target_pairs={{112,0},{0,16},{16,32},{32,48},{48,64},{64,80},{80,96},{96,112},{1... | collective-permute-start | bytes 14155784 | tf_op jit(solution)/shard_map/ppermute | solution.py:12
  308.5 2.1 copy-start.2
  314.4 232.8 %reduce-scatter.11.cloned.1.call-start = ((), (), s32[]{:S(2)}) async-start(), calls=%async_computation.8 | async-start | bytes 5013504 | tf_op jit(solution)/shard_map/reduce_scatter | solution.py:58
  314.4 120.4 %collective-permute-start.2 = (bf16[2048,1152]{1,0:T(8,128)(2,1)}, bf16[2048,1152]{1,0:T(8,128)(2,1)S(1)}, u32[]{:S(2)}, u32[]{:S(2)}) collective-permute-start(bf16[2048,1152]{1,0:T(8,128)(2,1)} %copy-done.2), channel_id=1, source_target_pairs={{112,0},{0,16},{16,32},{32,48},{48,64},{64,80},{80,96},{96,112},{1... | collective-permute-start | bytes 14155784 | tf_op jit(solution)/shard_map/ppermute | solution.py:12
  434.8 2.2 copy-start.4
  441.8 31.1 %collective-permute-start.3 = (f32[128,1152]{1,0:T(8,128)S(1)}, f32[128,1152]{1,0:T(8,128)}, u32[]{:S(2)}, u32[]{:S(2)}) collective-permute-start(f32[128,1152]{1,0:T(8,128)S(1)} %convert_element_type.57), channel_id=1, source_target_pairs={{112,0},{0,16},{16,32},{32,48},{48,64},{64,80},{80,96},{96,112},{1... | collective-permute-start | bytes 1769480 | tf_op jit(solution)/shard_map/ppermute | solution.py:12
  474.1 14.2 %collective-permute-start.4 = (f32[128,1152]{1,0:T(8,128)S(1)}, f32[128,1152]{1,0:T(8,128)}, u32[]{:S(2)}, u32[]{:S(2)}) collective-permute-start(f32[128,1152]{1,0:T(8,128)S(1)} %convert_add_fusion.2), channel_id=1, source_target_pairs={{112,0},{0,16},{16,32},{32,48},{48,64},{64,80},{80,96},{96,112},{1... | collective-permute-start | bytes 1769480 | tf_op jit(solution)/shard_map/ppermute | solution.py:12
  489.5 13.3 %collective-permute-start.5 = (f32[128,1152]{1,0:T(8,128)S(1)}, f32[128,1152]{1,0:T(8,128)}, u32[]{:S(2)}, u32[]{:S(2)}) collective-permute-start(f32[128,1152]{1,0:T(8,128)S(1)} %convert_add_fusion.1), channel_id=1, source_target_pairs={{112,0},{0,16},{16,32},{32,48},{48,64},{64,80},{80,96},{96,112},{1... | collective-permute-start | bytes 1769480 | tf_op jit(solution)/shard_map/ppermute | solution.py:12
  548.3 14.8 %copy-start.3 = (bf16[128,1152]{1,0:T(8,128)(2,1)S(1)}, bf16[128,1152]{1,0:T(8,128)(2,1)}, u32[]{:S(2)}) copy-start(bf16[128,1152]{1,0:T(8,128)(2,1)} %param.5) | copy-start | bytes 884740
  548.4 14.8 %collective-permute-start.6 = (f32[128,1152]{1,0:T(8,128)S(1)}, f32[128,1152]{1,0:T(8,128)S(1)}, u32[]{:S(2)}, u32[]{:S(2)}) collective-permute-start(f32[128,1152]{1,0:T(8,128)S(1)} %convert_add_fusion), channel_id=1, source_target_pairs={{48,0},{64,16},{80,32},{96,48},{112,64},{0,80},{16,96},{32,112},{4... | collective-permute-start | bytes 1769480 | tf_op jit(solution)/shard_map/ppermute | solution.py:12
Sparse Core Ops, SparseCore 0:
  11.0 59.2 all-gather.1
  78.4 92.9 reduce-scatter.4
  188.5 108.3 reduce-scatter.6
  314.5 109.9 reduce-scatter.8
  440.9 106.2 reduce-scatter.10
where the time goes:
time: 572 us; the launch traced here: 571 us
  waiting for transfers between devices  500 us (87%)
  matrix products  37.8 us (7%)
  between operations  15.2 us (3%)
  other arithmetic  10.9 us (2%)
    ppermute x7, waiting for transfers between devices, from_behind(): return lax.ppermute(block, axis, route)  398 us
    all_gather x1, waiting for transfers between devices, pool_rows(): return lax.all_gather(rows, 'group', axis=0, tiled=True)  57.7 us
    reduce_scatter x4, waiting for transfers between devices, local(): lax.psum_scatter(term.astype(jnp.bfloat16), 'group', scatter_dimension=0,...  44.3 us
    dot_general x4, matrix products, local(): term = scale * jnp.dot(slopes.T, ibf, preferred_element_type=jnp.float32)  14.7 us
    dot_general x4, matrix products, local(): jnp.dot(slopes, visiting, preferred_element_type=jnp.float32)  13.8 us
  transfers between devices with their start and end apart: 12, of which 9 were waited for; matrix products, arithmetic and copies ran while one was open for 6% of the time, Pallas kernels for 0%

commit v1 on v0

v1 whole, which is shorter than its diff:
```python
import functools

import jax
import jax.numpy as jnp
from jax import lax
from jax.experimental import pallas as pl
from jax.experimental.pallas import tpu as pltpu
from jax.sharding import PartitionSpec as P

MESH = pl.DeviceIdType.MESH
ROWS = 128
HALF = 64
WIDTH = 1152
BF = jnp.bfloat16
F32 = jnp.float32


def slot_at(k, h, j):
    return k * 4 + h * 2 + j


def kernel(
    scal, images, texts, grad_images, grad_texts,
    inormed, tnormed, inorm, tnorm,
    im, tb, di, pb,
    xr, zr, o0, o1, dr, dyr,
    sx, sz, sd, sy,
    send, im_r, tb_r, xr_r, zr_r, o0_r, o1_r, dr_r, dy_r,
):
    loop = lax.axis_index("loop")
    group = lax.axis_index("group")
    x = (group // 2) % 2 * 2 + loop // 4
    z = loop % 4
    y = group // 4
    core = group % 2

    def at(dx=0, dy=0, dz=0, dc=0):
        xx = (x + dx + 8) % 4
        yy = (y + dy + 4) % 4
        zz = (z + dz + 4) % 4
        return (xx % 2 * 4 + zz, yy * 4 + xx // 2 * 2 + (core + dc) % 2)

    barrier = pltpu.get_barrier_semaphore()
    partners = [at(dc=1)]
    for d in (1, 2, 3):
        partners += [at(dx=d), at(dy=d), at(dz=d)]
    for partner in partners:
        pl.semaphore_signal(barrier, inc=1, device_id=partner, device_id_type=MESH)

    def normalize(src, normed, norm):
        wide = src[...].astype(F32)
        n = jnp.sqrt(jnp.sum(wide * wide, axis=-1, keepdims=True) + 1e-06)
        out = wide / n
        normed[...] = out
        norm[...] = n
        return out.astype(BF)

    def part(ref, slot, count=1):
        return ref.at[pl.ds(pl.multiple_of(slot * HALF, HALF), HALF * count)]

    own_text = normalize(texts, tnormed, tnorm)
    tb[0:HALF] = own_text[0:HALF]
    tb[2 * HALF:3 * HALF] = own_text[HALF:]
    im[0, core] = normalize(images, inormed, inorm)

    pl.semaphore_wait(barrier, len(partners))

    pending = []

    def put(src, dst, recv, device, cond=None):
        sem = send.at[len(pending)]

        def make():
            return pltpu.make_async_remote_copy(
                src_ref=src(), dst_ref=dst(), send_sem=sem, recv_sem=recv(),
                device_id=device, device_id_type=MESH,
            )

        pending.append((make, cond))
        if cond is None:
            make().start()
        else:
            @pl.when(cond)
            def _():
                make().start()

    def got(dst, recv, cond=None):
        def wait():
            pltpu.make_async_remote_copy(
                src_ref=dst(), dst_ref=dst(), send_sem=send.at[0], recv_sem=recv(),
                device_id=at(dc=1), device_id_type=MESH,
            ).wait_recv()

        if cond is None:
            wait()
        else:
            @pl.when(cond)
            def _():
                wait()

    def put_slot(src, dst, device, cond=None):
        put(lambda: part(tb, src), lambda: part(tb, dst), lambda: tb_r.at[dst], device, cond)

    def got_slot(slot, cond=None):
        got(lambda: part(tb, slot), lambda: tb_r.at[slot], cond)

    wraps = [(z + k >= 4).astype(jnp.int32) for k in range(4)]
    wrapped = [(z < k).astype(jnp.int32) for k in range(4)]

    put_slot(0, slot_at(0, 0, 1), at(dx=2))
    for d in (1, 3):
        put_slot(0, 16 + d // 2, at(dx=d), z > 0)
    for k in (1, 3, 2):
        s = wraps[k]
        there = s * (17 + k) + (1 - s) * slot_at(k, 1, 0)
        put_slot(2, there, at(dz=k))
    for d in (1, 3, 2):
        put(lambda: im.at[0, core], lambda d=d: im.at[d, core], lambda d=d: im_r.at[d, core], at(dy=d))
    put(lambda: im.at[0, core], lambda: im.at[0, core], lambda: im_r.at[0, core], at(dc=1))
    for k in (1, 3, 2):
        put_slot(0, slot_at(k, 0, 0), at(dz=k), wraps[k] == 0)
    put_slot(2, slot_at(0, 1, 1), at(dx=2))

    got_slot(slot_at(0, 0, 1))
    for k in (1, 3, 2):
        put_slot(slot_at(0, 0, 1), slot_at(k, 0, 1), at(dz=k), wraps[k] == 0)

    def forward_x(k):
        s = wrapped[k]
        here = s * (17 + k) + (1 - s) * slot_at(k, 1, 0)
        got_slot(here)
        put_slot(here, slot_at(k, 1, 1), at(dx=s + 2))
        put_slot(here, slot_at(k, 1, 0), at(dx=1), s == 1)

    forward_x(1)
    for d in (1, 3):
        got_slot(16 + d // 2, z > 0)
        for k in (3, 2, 1):
            put_slot(16 + d // 2, slot_at(k, 0, d // 2), at(dz=k), wraps[k] == 1)
    forward_x(3)
    forward_x(2)

    def relay_image(d):
        got(lambda: im.at[d, core], lambda: im_r.at[d, core])
        put(lambda: im.at[d, core], lambda: im.at[d, core], lambda: im_r.at[d, core], at(dc=1))

    for d in (1, 3, 2):
        relay_image(d)
    for d in (0, 1, 3, 2):
        got(lambda d=d: im.at[d, 1 - core], lambda d=d: im_r.at[d, 1 - core])

    scale = scal[0]
    shift = scal[1]

    def chunk(k, first):
        rows = pl.ds(k * 4 * HALF, 4 * HALF)
        t = tb[rows]
        i = im[...].reshape(8 * ROWS, WIDTH)
        logits = scale * lax.dot_general(t, i, (((1,), (1,)), ((), ())), preferred_element_type=F32) + shift
        if k == 0:
            r = lax.broadcasted_iota(jnp.int32, logits.shape, 0)
            c = lax.broadcasted_iota(jnp.int32, logits.shape, 1)
            own = r // (2 * HALF) * HALF + r % HALF + core * ROWS
            positive = (c == own) & (r // HALF % 2 == 0)
            signs = jnp.where(positive, 1.0, -1.0).astype(F32)
            slopes = -signs / (1.0 + jnp.exp(signs * logits))
        else:
            slopes = 1.0 / (1.0 + jnp.exp(-logits))
        slopes = slopes.astype(BF)
        pb[rows] = (scale * jnp.dot(slopes, i, preferred_element_type=F32)).astype(BF)
        term = lax.dot_general(slopes, t, (((0,), (0,)), ((), ())), preferred_element_type=F32)
        if first:
            di[...] = term
        else:
            di[...] += term

    got_slot(slot_at(0, 1, 1))
    chunk(0, True)
    put(lambda: part(pb, slot_at(0, 1, 1)), lambda: o1.at[0], lambda: o1_r.at[0], at(dx=2))

    for k in (1, 3, 2):
        s = wrapped[k]
        got_slot(slot_at(k, 0, 0))
        got_slot(slot_at(k, 0, 1))
        got_slot(slot_at(k, 1, 0), s == 1)
        got_slot(slot_at(k, 1, 1))
        chunk(k, False)
        put(lambda k=k: part(pb, slot_at(k, 0, 0), 2), lambda k=k: xr.at[k - 1], lambda k=k: xr_r.at[k - 1], at(dz=-k))
        put(lambda k=k: part(pb, slot_at(k, 1, 1)), lambda k=k: zr.at[k - 1, 1], lambda k=k: zr_r.at[k - 1, 1], at(dx=-s - 2))
        put(lambda k=k: part(pb, slot_at(k, 1, 0)), lambda k=k: zr.at[k - 1, 0], lambda k=k: zr_r.at[k - 1, 0], at(dx=-1), s == 1)

    for d in (1, 3, 2, 0):
        rows = pl.ds(pl.multiple_of(d * 2 * ROWS + (1 - core) * ROWS, ROWS), ROWS)
        sd[d] = (scale * di[rows]).astype(BF)
        put(lambda d=d: sd.at[d], lambda d=d: dr.at[d], lambda d=d: dr_r.at[d], at(dc=1))

    def mine(d):
        rows = pl.ds(pl.multiple_of(d * 2 * ROWS + core * ROWS, ROWS), ROWS)
        got(lambda: dr.at[d], lambda: dr_r.at[d])
        return scale * di[rows] + dr[d].astype(F32)

    for d in (1, 3, 2):
        sy[d - 1] = mine(d).astype(BF)
        put(lambda d=d: sy.at[d - 1], lambda d=d: dyr.at[d - 1], lambda d=d: dy_r.at[d - 1], at(dy=-d))

    def value(slot):
        return part(pb, slot)[...].astype(F32)

    for k in (1, 3, 2):
        s = wrapped[k]
        got(lambda k=k: zr.at[k - 1, 1], lambda k=k: zr_r.at[k - 1, 1])
        got(lambda k=k: zr.at[k - 1, 0], lambda k=k: zr_r.at[k - 1, 0], s == 1)

        @pl.when(s == 1)
        def _():
            sz[k - 1] = (zr[k - 1, 1].astype(F32) + zr[k - 1, 0].astype(F32)).astype(BF)

        @pl.when(s == 0)
        def _():
            sz[k - 1] = (zr[k - 1, 1].astype(F32) + value(slot_at(k, 1, 0))).astype(BF)

        put(lambda k=k: sz.at[k - 1], lambda k=k: o1.at[k], lambda k=k: o1_r.at[k], at(dz=-k))

    for k in (1, 3, 2):
        got(lambda k=k: xr.at[k - 1], lambda k=k: xr_r.at[k - 1])

    def column(j, wrap):
        total = None
        for k in (1, 2, 3):
            term = xr[k - 1, pl.ds(j * HALF, HALF)].astype(F32)
            term = jnp.where(wraps[k] == wrap, term, 0.0)
            total = term if total is None else total + term
        return total

    sx[1] = (column(1, 0) + value(slot_at(0, 0, 1))).astype(BF)
    put(lambda: sx.at[1], lambda: o0.at[1], lambda: o0_r.at[1], at(dx=-2))
    for d in (1, 3):
        @pl.when(z > 0)
        def _():
            sx[d - 1] = column(d // 2, 1).astype(BF)

        put(lambda d=d: sx.at[d - 1], lambda d=d: o0.at[d - 1], lambda d=d: o0_r.at[d - 1], at(dx=-d), z > 0)

    def unnormalize(normed, norm, upstream):
        inner = jnp.sum(normed * upstream, axis=-1, keepdims=True)
        return (upstream - normed * inner) / norm

    total = mine(0)
    for d in (1, 3, 2):
        got(lambda d=d: dyr.at[d - 1], lambda d=d: dy_r.at[d - 1])
        total = total + dyr[d - 1].astype(F32)
    grad_images[...] = unnormalize(inormed[...], inorm[...], total)

    lower = column(0, 0) + value(slot_at(0, 0, 0))
    got(lambda: o0.at[1], lambda: o0_r.at[1])
    lower = lower + o0[1].astype(F32)
    for d in (1, 3):
        got(lambda d=d: o0.at[d - 1], lambda d=d: o0_r.at[d - 1], z > 0)
        lower = lower + jnp.where(z > 0, o0[d - 1].astype(F32), 0.0)
    upper = value(slot_at(0, 1, 0))
    for k in (0, 1, 3, 2):
        got(lambda k=k: o1.at[k], lambda k=k: o1_r.at[k])
        upper = upper + o1[k].astype(F32)
    grad_texts[0:HALF] = unnormalize(tnormed[0:HALF], tnorm[0:HALF], lower)
    grad_texts[HALF:] = unnormalize(tnormed[HALF:], tnorm[HALF:], upper)

    for make, cond in pending:
        if cond is None:
            make().wait_send()
        else:
            @pl.when(cond)
            def _():
                make().wait_send()


def local(images, texts, logit_scale, bias):
    vmem = pl.BlockSpec(memory_space=pltpu.VMEM)
    dma = pltpu.SemaphoreType.DMA
    return pl.pallas_call(
        kernel,
        out_shape=[jax.ShapeDtypeStruct((ROWS, WIDTH), F32)] * 2,
        in_specs=[pl.BlockSpec(memory_space=pltpu.SMEM), vmem, vmem],
        out_specs=[vmem, vmem],
        scratch_shapes=[
            pltpu.VMEM((ROWS, WIDTH), F32),
            pltpu.VMEM((ROWS, WIDTH), F32),
            pltpu.VMEM((ROWS, 1), F32),
            pltpu.VMEM((ROWS, 1), F32),
            pltpu.VMEM((4, 2, ROWS, WIDTH), BF),
            pltpu.VMEM((21 * HALF, WIDTH), BF),
            pltpu.VMEM((8 * ROWS, WIDTH), F32),
            pltpu.VMEM((16 * HALF, WIDTH), BF),
            pltpu.VMEM((3, 2 * HALF, WIDTH), BF),
            pltpu.VMEM((3, 2, HALF, WIDTH), BF),
            pltpu.VMEM((3, HALF, WIDTH), BF),
            pltpu.VMEM((4, HALF, WIDTH), BF),
            pltpu.VMEM((4, ROWS, WIDTH), BF),
            pltpu.VMEM((3, ROWS, WIDTH), BF),
            pltpu.VMEM((3, HALF, WIDTH), BF),
            pltpu.VMEM((3, HALF, WIDTH), BF),
            pltpu.VMEM((4, ROWS, WIDTH), BF),
            pltpu.VMEM((3, ROWS, WIDTH), BF),
            dma((64,)),
            dma((4, 2)),
            dma((21,)),
            dma((3,)),
            dma((3, 2)),
            dma((3,)),
            dma((4,)),
            dma((4,)),
            dma((3,)),
        ],
        compiler_params=pltpu.CompilerParams(
            collective_id=0, has_side_effects=True, vmem_limit_bytes=56 * 2**20
        ),
        name="pair_grads",
    )(jnp.concatenate([logit_scale, bias]), images, texts)


def solution(mesh):
    in_specs = (P(("loop", "group"), None), P(("loop", "group"), None), P(), P())
    out_specs = (P(("loop", "group"), None), P(("loop", "group"), None))
    return jax.shard_map(local, mesh=mesh, in_specs=in_specs, out_specs=out_specs, check_vma=False)
```

time: 572 us -> 64.3 us (0.11)
  the two profiles are of different devices: /device:TPU:32 before, /device:TPU:1 now
where the time goes in v1:
time: 64.3 us; the launch traced here: 64.1 us
  Pallas kernels  58.8 us (91%)
  local copies, waits for them, and re-layouts  2.8 us (4%)
  between operations  1.94 us (3%)
    pallas_call x1, Pallas kernels, local(): pl.pallas_call(kernel, out_shape=[jax.ShapeDtypeStruct((ROWS, WIDTH), F32...  58.8 us
    unnamed x4, local copies, waits for them, and re-layouts  2.8 us

profile of v1, /device:TPU:1, one launch (start us, length us, event | category | flops | bytes accessed | tf_op | source)
XLA Modules:
  0.0 64.1 jit_solution(16470986203915613256)
XLA Ops:
  1.9 0.6 pad_maximum_fusion.scal
  2.5 58.8 %pair_grads.1 = (f32[128,1152]{1,0:T(8,128)}, f32[128,1152]{1,0:T(8,128)}) custom-call(f32[2]{0:T(128)} %pad_maximum_fusion.scal, bf16[128,1152]{1,0:T(8,128)(2,1)} %images.1, bf16[128,1152]{1,0:T(8,128)(2,1)} %texts.1), custom_call_target="tpu_custom_call" | custom-call | tf_op jit(solution)/shard_map/pair_grads/pallas_call | solution.py:279
  61.3 0.0 copy-start
  61.3 2.0 %copy.10 = f32[128,1152]{1,0:T(8,128)} copy(f32[128,1152]{1,0:T(8,128)} %get-tuple-element.4) | data formatting | bytes 1179648
  63.3 0.0 copy-done
  63.3 0.8 %copy.11 = f32[128,1152]{1,0:T(8,128)} copy(f32[128,1152]{1,0:T(8,128)S(1)} %copy-done) | data formatting | bytes 1179648
Async XLA Ops:
  61.3 2.0 %copy-start = (f32[128,1152]{1,0:T(8,128)S(1)}, f32[128,1152]{1,0:T(8,128)}, u32[]{:S(2)}) copy-start(f32[128,1152]{1,0:T(8,128)} %get-tuple-element.5) | copy-start | bytes 1769476

commit v2 on v1

v2 whole, which is shorter than its diff:
```python
import functools

import jax
import jax.numpy as jnp
from jax import lax
from jax.experimental import pallas as pl
from jax.experimental.pallas import tpu as pltpu
from jax.sharding import PartitionSpec as P

MESH = pl.DeviceIdType.MESH
ROWS = 128
HALF = 64
WIDTH = 1152
BF = jnp.bfloat16
F32 = jnp.float32


CHUNK_AT = {2: 0, 3: 1, 0: 2, 1: 3}
IMAGE_AT = {0: 0, 1: 1, 3: 2, 2: 3}
EARLY = 6 * ROWS


def slot_at(k, h, j):
    return CHUNK_AT[k] * 4 + h * 2 + j


def kernel(
    logit_scale, bias, images_hbm, texts_hbm, grad_images, grad_texts,
    images, texts,
    inormed, tnormed, inorm, tnorm,
    im, tb, di, pt, pb,
    xr, zr, o0, o1, dr, dyr,
    sx, sz, sd, sy,
    moved, send, im_r, tb_r, xr_r, zr_r, o0_r, o1_r, dr_r, dy_r,
):
    loop = lax.axis_index("loop")
    group = lax.axis_index("group")
    x = (group // 2) % 2 * 2 + loop // 4
    z = loop % 4
    y = group // 4
    core = group % 2

    def at(dx=0, dy=0, dz=0, dc=0):
        xx = (x + dx + 8) % 4
        yy = (y + dy + 4) % 4
        zz = (z + dz + 4) % 4
        return (xx % 2 * 4 + zz, yy * 4 + xx // 2 * 2 + (core + dc) % 2)

    barrier = pltpu.get_barrier_semaphore()
    partners = [at(dc=1)]
    for d in (1, 2, 3):
        partners += [at(dx=d), at(dy=d), at(dz=d)]
    for partner in partners:
        pl.semaphore_signal(barrier, inc=1, device_id=partner, device_id_type=MESH)

    loads = [
        pltpu.make_async_copy(texts_hbm, texts, moved.at[0]),
        pltpu.make_async_copy(images_hbm, images, moved.at[1]),
    ]
    for load in loads:
        load.start()

    def normalize(src, normed, norm):
        wide = src[...].astype(F32)
        n = jnp.sqrt(jnp.sum(wide * wide, axis=-1, keepdims=True) + 1e-06)
        out = wide / n
        normed[...] = out
        norm[...] = n
        return out.astype(BF)

    def part(ref, slot, count=1):
        return ref.at[pl.ds(pl.multiple_of(slot * HALF, HALF), HALF * count)]

    loads[0].wait()
    own_text = normalize(texts, tnormed, tnorm)
    part(tb, slot_at(0, 0, 0))[...] = own_text[0:HALF]
    part(tb, slot_at(0, 1, 0))[...] = own_text[HALF:]
    loads[1].wait()
    im[0, core] = normalize(images, inormed, inorm)

    pl.semaphore_wait(barrier, len(partners))

    pending = []

    def put(src, dst, recv, device, cond=None):
        sem = send.at[len(pending)]

        def make():
            return pltpu.make_async_remote_copy(
                src_ref=src(), dst_ref=dst(), send_sem=sem, recv_sem=recv(),
                device_id=device, device_id_type=MESH,
            )

        pending.append((make, cond))
        if cond is None:
            make().start()
        else:
            @pl.when(cond)
            def _():
                make().start()

    def got(dst, recv, cond=None):
        def wait():
            pltpu.make_async_remote_copy(
                src_ref=dst(), dst_ref=dst(), send_sem=send.at[0], recv_sem=recv(),
                device_id=at(dc=1), device_id_type=MESH,
            ).wait_recv()

        if cond is None:
            wait()
        else:
            @pl.when(cond)
            def _():
                wait()

    def put_slot(src, dst, device, cond=None):
        put(lambda: part(tb, src), lambda: part(tb, dst), lambda: tb_r.at[dst], device, cond)

    def got_slot(slot, cond=None):
        got(lambda: part(tb, slot), lambda: tb_r.at[slot], cond)

    wraps = [(z + k >= 4).astype(jnp.int32) for k in range(4)]
    wrapped = [(z < k).astype(jnp.int32) for k in range(4)]

    own_low, own_high = slot_at(0, 0, 0), slot_at(0, 1, 0)

    def along_z_high(k):
        s = wraps[k]
        put_slot(own_high, s * (17 + k) + (1 - s) * slot_at(k, 1, 0), at(dz=k))

    def along_z_low(k):
        put_slot(own_low, slot_at(k, 0, 0), at(dz=k), wraps[k] == 0)

    def relay_z_near(order):
        for d in (1, 3):
            got_slot(16 + d // 2, z > 0)
            for k in order:
                put_slot(16 + d // 2, slot_at(k, 0, d // 2), at(dz=k), wraps[k] == 1)

    def relay_z_far(order):
        got_slot(slot_at(0, 0, 1))
        for k in order:
            put_slot(slot_at(0, 0, 1), slot_at(k, 0, 1), at(dz=k), wraps[k] == 0)

    def relay_x(k):
        s = wrapped[k]
        here = s * (17 + k) + (1 - s) * slot_at(k, 1, 0)
        got_slot(here)
        put_slot(here, slot_at(k, 1, 1), at(dx=s + 2))
        put_slot(here, slot_at(k, 1, 0), at(dx=1), s == 1)

    def send_image(d):
        a = IMAGE_AT[d]
        put(lambda: im.at[0, core], lambda: im.at[a, core], lambda: im_r.at[a, core], at(dy=d))

    def relay_image(d):
        a = IMAGE_AT[d]
        if d:
            got(lambda: im.at[a, core], lambda: im_r.at[a, core])
        put(lambda: im.at[a, core], lambda: im.at[a, core], lambda: im_r.at[a, core], at(dc=1))

    def got_image(d):
        a = IMAGE_AT[d]
        got(lambda: im.at[a, 1 - core], lambda: im_r.at[a, 1 - core])

    scale = logit_scale[0]
    shift = bias[0]

    def early(k, first):
        base = CHUNK_AT[k] * 4 * HALF
        rows = pl.ds(base, 4 * HALF)
        t = tb[rows]
        i = im[0:3].reshape(EARLY, WIDTH)
        logits = scale * lax.dot_general(t, i, (((1,), (1,)), ((), ())), preferred_element_type=F32) + shift
        if k == 0:
            r = lax.broadcasted_iota(jnp.int32, logits.shape, 0)
            c = lax.broadcasted_iota(jnp.int32, logits.shape, 1)
            own = r // (2 * HALF) * HALF + r % HALF + core * ROWS
            positive = (c == own) & (r // HALF % 2 == 0)
            signs = jnp.where(positive, 1.0, -1.0).astype(F32)
            slopes = -signs / (1.0 + jnp.exp(signs * logits))
        else:
            slopes = 1.0 / (1.0 + jnp.exp(-logits))
        slopes = slopes.astype(BF)
        pt[rows] = jnp.dot(slopes, i, preferred_element_type=F32)
        term = lax.dot_general(slopes, t, (((0,), (0,)), ((), ())), preferred_element_type=F32)
        if first:
            di[0:EARLY] = term
        else:
            di[0:EARLY] += term

    def late(ks, first):
        rows = pl.ds(CHUNK_AT[ks[0]] * 4 * HALF, 4 * HALF * len(ks))
        t = tb[rows]
        i = im[3].reshape(2 * ROWS, WIDTH)
        logits = scale * lax.dot_general(i, t, (((1,), (1,)), ((), ())), preferred_element_type=F32) + shift
        slopes = (1.0 / (1.0 + jnp.exp(-logits))).astype(BF)
        term = lax.dot_general(slopes, i, (((0,), (0,)), ((), ())), preferred_element_type=F32)
        pb[rows] = (scale * (pt[rows] + term)).astype(BF)
        term = jnp.dot(slopes, t, preferred_element_type=F32)
        if first:
            di[EARLY:] = term
        else:
            di[EARLY:] += term

    def value(slot):
        return part(pb, slot)[...].astype(F32)

    def got_chunk(k):
        if k == 0:
            got_slot(slot_at(0, 1, 1))
            return
        got_slot(slot_at(k, 0, 0))
        got_slot(slot_at(k, 0, 1))
        got_slot(slot_at(k, 1, 0), wrapped[k] == 1)
        got_slot(slot_at(k, 1, 1))

    def send_chunk(k):
        if k == 0:
            put(lambda: part(pb, slot_at(0, 1, 1)), lambda: o1.at[0], lambda: o1_r.at[0], at(dx=2))
            return
        s = wrapped[k]
        put(lambda: part(pb, slot_at(k, 1, 1)), lambda: zr.at[k - 1, 1], lambda: zr_r.at[k - 1, 1], at(dx=-s - 2))
        put(lambda: part(pb, slot_at(k, 1, 0)), lambda: zr.at[k - 1, 0], lambda: zr_r.at[k - 1, 0], at(dx=-1), s == 1)
        put(lambda: part(pb, slot_at(k, 0, 0), 2), lambda: xr.at[k - 1], lambda: xr_r.at[k - 1], at(dz=-k))

    def collect_z(k):
        s = wrapped[k]
        got(lambda: zr.at[k - 1, 1], lambda: zr_r.at[k - 1, 1])
        got(lambda: zr.at[k - 1, 0], lambda: zr_r.at[k - 1, 0], s == 1)

        @pl.when(s == 1)
        def _():
            sz[k - 1] = (zr[k - 1, 1].astype(F32) + zr[k - 1, 0].astype(F32)).astype(BF)

        @pl.when(s == 0)
        def _():
            sz[k - 1] = (zr[k - 1, 1].astype(F32) + value(slot_at(k, 1, 0))).astype(BF)

        put(lambda: sz.at[k - 1], lambda: o1.at[k], lambda: o1_r.at[k], at(dz=-k))

    def di_rows(d, half):
        return pl.ds(pl.multiple_of(IMAGE_AT[d] * 2 * ROWS + half * ROWS, ROWS), ROWS)

    def swap_images():
        for d in (2, 1, 3, 0):
            sd[d] = (scale * di[di_rows(d, 1 - core)]).astype(BF)
            put(lambda d=d: sd.at[d], lambda d=d: dr.at[d], lambda d=d: dr_r.at[d], at(dc=1))

    def mine(d):
        got(lambda: dr.at[d], lambda: dr_r.at[d])
        return scale * di[di_rows(d, core)] + dr[d].astype(F32)

    def return_images():
        for d in (2, 1, 3):
            sy[d - 1] = mine(d).astype(BF)
            put(lambda d=d: sy.at[d - 1], lambda d=d: dyr.at[d - 1], lambda d=d: dy_r.at[d - 1], at(dy=-d))

    def column(j, wrap):
        total = None
        for k in (1, 2, 3):
            term = xr[k - 1, pl.ds(j * HALF, HALF)].astype(F32)
            term = jnp.where(wraps[k] == wrap, term, 0.0)
            total = term if total is None else total + term
        return total

    def collect_x():
        for k in (1, 3, 2):
            got(lambda k=k: xr.at[k - 1], lambda k=k: xr_r.at[k - 1])
        sx[1] = (column(1, 0) + value(slot_at(0, 0, 1))).astype(BF)
        put(lambda: sx.at[1], lambda: o0.at[1], lambda: o0_r.at[1], at(dx=-2))
        for d in (1, 3):
            @pl.when(z > 0)
            def _():
                sx[d - 1] = column(d // 2, 1).astype(BF)

            put(lambda d=d: sx.at[d - 1], lambda d=d: o0.at[d - 1], lambda d=d: o0_r.at[d - 1], at(dx=-d), z > 0)

    def unnormalize(normed, norm, upstream):
        inner = jnp.sum(normed * upstream, axis=-1, keepdims=True)
        return (upstream - normed * inner) / norm

    for d in (1, 3, 2):
        send_image(d)
    along_z_high(2)
    along_z_high(1)
    along_z_high(3)
    for d in (1, 3):
        put_slot(own_low, 16 + d // 2, at(dx=d), z > 0)
    put_slot(own_low, slot_at(0, 0, 1), at(dx=2))
    along_z_low(2)
    put_slot(own_high, slot_at(0, 1, 1), at(dx=2))
    along_z_low(3)
    relay_image(0)
    relay_x(3)
    relay_z_near((3, 1, 2))
    relay_z_far((2, 1, 3))
    along_z_low(1)
    relay_image(1)
    relay_image(3)
    relay_x(2)
    relay_image(2)
    relay_x(1)
    got_chunk(0)
    for d in (0, 1, 3):
        got_image(d)
    early(0, True)
    got_chunk(3)
    early(3, False)
    got_chunk(2)
    early(2, False)
    got_image(2)
    late((2, 3), True)
    send_chunk(2)
    send_chunk(3)
    got_chunk(1)
    early(1, False)
    late((0, 1), False)
    send_chunk(0)
    send_chunk(1)
    swap_images()
    return_images()
    collect_z(2)
    collect_x()
    collect_z(1)
    collect_z(3)

    total = mine(0)
    for d in (1, 3, 2):
        got(lambda d=d: dyr.at[d - 1], lambda d=d: dy_r.at[d - 1])
        total = total + dyr[d - 1].astype(F32)
    grad_images[...] = unnormalize(inormed[...], inorm[...], total)

    lower = column(0, 0) + value(slot_at(0, 0, 0))
    got(lambda: o0.at[1], lambda: o0_r.at[1])
    lower = lower + o0[1].astype(F32)
    for d in (1, 3):
        got(lambda d=d: o0.at[d - 1], lambda d=d: o0_r.at[d - 1], z > 0)
        lower = lower + jnp.where(z > 0, o0[d - 1].astype(F32), 0.0)
    upper = value(slot_at(0, 1, 0))
    for k in (0, 1, 3, 2):
        got(lambda k=k: o1.at[k], lambda k=k: o1_r.at[k])
        upper = upper + o1[k].astype(F32)
    grad_texts[0:HALF] = unnormalize(tnormed[0:HALF], tnorm[0:HALF], lower)
    grad_texts[HALF:] = unnormalize(tnormed[HALF:], tnorm[HALF:], upper)

    for make, cond in pending:
        if cond is None:
            make().wait_send()
        else:
            @pl.when(cond)
            def _():
                make().wait_send()


def local(images, texts, logit_scale, bias):
    hbm = pl.BlockSpec(memory_space=pl.ANY)
    vmem = pl.BlockSpec(memory_space=pltpu.VMEM)
    smem = pl.BlockSpec(memory_space=pltpu.SMEM)
    dma = pltpu.SemaphoreType.DMA
    return pl.pallas_call(
        kernel,
        out_shape=[pltpu.VMEM((ROWS, WIDTH), F32)] * 2,
        in_specs=[smem, smem, hbm, hbm],
        out_specs=[vmem, vmem],
        scratch_shapes=[
            pltpu.VMEM((ROWS, WIDTH), BF),
            pltpu.VMEM((ROWS, WIDTH), BF),
            pltpu.VMEM((ROWS, WIDTH), F32),
            pltpu.VMEM((ROWS, WIDTH), F32),
            pltpu.VMEM((ROWS, 1), F32),
            pltpu.VMEM((ROWS, 1), F32),
            pltpu.VMEM((4, 2, ROWS, WIDTH), BF),
            pltpu.VMEM((21 * HALF, WIDTH), BF),
            pltpu.VMEM((8 * ROWS, WIDTH), F32),
            pltpu.VMEM((16 * HALF, WIDTH), F32),
            pltpu.VMEM((16 * HALF, WIDTH), BF),
            pltpu.VMEM((3, 2 * HALF, WIDTH), BF),
            pltpu.VMEM((3, 2, HALF, WIDTH), BF),
            pltpu.VMEM((3, HALF, WIDTH), BF),
            pltpu.VMEM((4, HALF, WIDTH), BF),
            pltpu.VMEM((4, ROWS, WIDTH), BF),
            pltpu.VMEM((3, ROWS, WIDTH), BF),
            pltpu.VMEM((3, HALF, WIDTH), BF),
            pltpu.VMEM((3, HALF, WIDTH), BF),
            pltpu.VMEM((4, ROWS, WIDTH), BF),
            pltpu.VMEM((3, ROWS, WIDTH), BF),
            dma((2,)),
            dma((64,)),
            dma((4, 2)),
            dma((21,)),
            dma((3,)),
            dma((3, 2)),
            dma((3,)),
            dma((4,)),
            dma((4,)),
            dma((3,)),
        ],
        compiler_params=pltpu.CompilerParams(
            collective_id=0, has_side_effects=True, vmem_limit_bytes=56 * 2**20
        ),
        name="pair_grads",
    )(logit_scale, bias, images, texts)


def solution(mesh):
    in_specs = (P(("loop", "group"), None), P(("loop", "group"), None), P(), P())
    out_specs = (P(("loop", "group"), None), P(("loop", "group"), None))
    return jax.shard_map(local, mesh=mesh, in_specs=in_specs, out_specs=out_specs, check_vma=False)
```

time: 64.3 us -> 58.7 us (0.913)
  the two profiles are of different devices: /device:TPU:1 before, /device:TPU:32 now
where the time goes in v2:
time: 58.7 us; the launch traced here: 58 us
  Pallas kernels  54.4 us (93%)
  between operations  1.93 us (3%)
  local copies, waits for them, and re-layouts  1.63 us (3%)
    pallas_call x1, Pallas kernels, local(): pl.pallas_call(kernel, out_shape=[pltpu.VMEM((ROWS, WIDTH), F32)] * 2, in...  54.4 us
    unnamed x2, local copies, waits for them, and re-layouts  1.63 us

profile of v2, /device:TPU:32, one launch (start us, length us, event | category | flops | bytes accessed | tf_op | source)
XLA Modules:
  0.0 58.0 jit_solution(5301090857332446951)
XLA Ops:
  1.9 54.4 %pair_grads.1 = (f32[128,1152]{1,0:T(8,128)S(1)}, f32[128,1152]{1,0:T(8,128)S(1)}) custom-call(f32[1]{0:T(128)S(6)} %copy.10.logit_scale, f32[1]{0:T(128)S(6)} %copy.11.bias, bf16[128,1152]{1,0:T(8,128)(2,1)} %images_hbm.1, bf16[128,1152]{1,0:T(8,128)(2,1)} %texts_hbm.1), custom_call_target="tpu_custom_call" | custom-call | tf_op jit(solution)/shard_map/pair_grads/pallas_call | solution.py:361
  56.3 0.8 %copy.8 = f32[128,1152]{1,0:T(8,128)} copy(f32[128,1152]{1,0:T(8,128)S(1)} %get-tuple-element.2) | data formatting | bytes 1179648
  57.2 0.8 %copy.9 = f32[128,1152]{1,0:T(8,128)} copy(f32[128,1152]{1,0:T(8,128)S(1)} %get-tuple-element.3) | data formatting | bytes 1179648

commit v3 on v2

--- a/solution.py
+++ b/solution.py
@@ -10,6 +10,7 @@
 MESH = pl.DeviceIdType.MESH
 ROWS = 128
 HALF = 64
+QUARTER = 32
 WIDTH = 1152
 BF = jnp.bfloat16
 F32 = jnp.float32
@@ -30,8 +31,8 @@
     inormed, tnormed, inorm, tnorm,
     im, tb, di, pt, pb,
     xr, zr, o0, o1, dr, dyr,
-    sx, sz, sd, sy,
-    moved, send, im_r, tb_r, xr_r, zr_r, o0_r, o1_r, dr_r, dy_r,
+    sx, sz, sd, sy, sf, o2,
+    o2_r, moved, send, im_h, im_r, tb_r, xr_r, zr_r, o0_r, o1_r, dr_r, dy_r,
 ):
     loop = lax.axis_index("loop")
     group = lax.axis_index("group")
@@ -81,9 +82,10 @@
     pl.semaphore_wait(barrier, len(partners))
 
     pending = []
+    numbers = iter(range(64))
 
     def put(src, dst, recv, device, cond=None):
-        sem = send.at[len(pending)]
+        sem = send.at[next(numbers)]
 
         def make():
             return pltpu.make_async_remote_copy(
@@ -99,6 +101,17 @@
             def _():
                 make().start()
 
+    def drain(count):
+        for make, cond in pending[:count]:
+            if cond is None:
+                make().wait_send()
+            else:
+                @pl.when(cond)
+                def _():
+                    make().wait_send()
+
+        del pending[:count]
+
     def got(dst, recv, cond=None):
         def wait():
             pltpu.make_async_remote_copy(
@@ -131,11 +144,10 @@
     def along_z_low(k):
         put_slot(own_low, slot_at(k, 0, 0), at(dz=k), wraps[k] == 0)
 
-    def relay_z_near(order):
-        for d in (1, 3):
-            got_slot(16 + d // 2, z > 0)
-            for k in order:
-                put_slot(16 + d // 2, slot_at(k, 0, d // 2), at(dz=k), wraps[k] == 1)
+    def relay_z_near(d, order):
+        got_slot(16 + d // 2, z > 0)
+        for k in order:
+            put_slot(16 + d // 2, slot_at(k, 0, d // 2), at(dz=k), wraps[k] == 1)
 
     def relay_z_far(order):
         got_slot(slot_at(0, 0, 1))
@@ -149,19 +161,29 @@
         put_slot(here, slot_at(k, 1, 1), at(dx=s + 2))
         put_slot(here, slot_at(k, 1, 0), at(dx=1), s == 1)
 
-    def send_image(d):
+    def send_image(d, h):
         a = IMAGE_AT[d]
-        put(lambda: im.at[0, core], lambda: im.at[a, core], lambda: im_r.at[a, core], at(dy=d))
+        rows = pl.ds(h * HALF, HALF)
+        put(lambda: im.at[0, core, rows], lambda: im.at[a, core, rows], lambda: im_h.at[a, h], at(dy=d))
+
+    def forward_image(d):
+        a, b = IMAGE_AT[d], IMAGE_AT[2]
+        h = d // 2
+        rows = pl.ds(h * HALF, HALF)
+        got(lambda: im.at[a, core, rows], lambda: im_h.at[a, h])
+        put(lambda: im.at[a, core, rows], lambda: im.at[b, core, rows], lambda: im_h.at[b, h], at(dy=d))
 
     def relay_image(d):
         a = IMAGE_AT[d]
-        if d:
-            got(lambda: im.at[a, core], lambda: im_r.at[a, core])
-        put(lambda: im.at[a, core], lambda: im.at[a, core], lambda: im_r.at[a, core], at(dc=1))
+        for h in (0, 1):
+            if d == 2 or d and h != d // 2:
+                rows = pl.ds(h * HALF, HALF)
+                got(lambda: im.at[a, core, rows], lambda: im_h.at[a, h])
+        put(lambda: im.at[a, core], lambda: im.at[a, core], lambda: im_r.at[a], at(dc=1))
 
     def got_image(d):
         a = IMAGE_AT[d]
-        got(lambda: im.at[a, 1 - core], lambda: im_r.at[a, 1 - core])
+        got(lambda: im.at[a, 1 - core], lambda: im_r.at[a])
 
     scale = logit_scale[0]
     shift = bias[0]
@@ -215,14 +237,18 @@
         got_slot(slot_at(k, 1, 0), wrapped[k] == 1)
         got_slot(slot_at(k, 1, 1))
 
-    def send_chunk(k):
+    def send_chunk(k, order):
         if k == 0:
             put(lambda: part(pb, slot_at(0, 1, 1)), lambda: o1.at[0], lambda: o1_r.at[0], at(dx=2))
             return
         s = wrapped[k]
-        put(lambda: part(pb, slot_at(k, 1, 1)), lambda: zr.at[k - 1, 1], lambda: zr_r.at[k - 1, 1], at(dx=-s - 2))
-        put(lambda: part(pb, slot_at(k, 1, 0)), lambda: zr.at[k - 1, 0], lambda: zr_r.at[k - 1, 0], at(dx=-1), s == 1)
-        put(lambda: part(pb, slot_at(k, 0, 0), 2), lambda: xr.at[k - 1], lambda: xr_r.at[k - 1], at(dz=-k))
+        for which in order:
+            if which == "1":
+                put(lambda: part(pb, slot_at(k, 1, 1)), lambda: zr.at[k - 1, 1], lambda: zr_r.at[k - 1, 1], at(dx=-s - 2))
+            elif which == "0":
+                put(lambda: part(pb, slot_at(k, 1, 0)), lambda: zr.at[k - 1, 0], lambda: zr_r.at[k - 1, 0], at(dx=-1), s == 1)
+            else:
+                put(lambda: part(pb, slot_at(k, 0, 0), 2), lambda: xr.at[k - 1], lambda: xr_r.at[k - 1], at(dz=-k))
 
     def collect_z(k):
         s = wrapped[k]
@@ -231,12 +257,23 @@
 
         @pl.when(s == 1)
         def _():
-            sz[k - 1] = (zr[k - 1, 1].astype(F32) + zr[k - 1, 0].astype(F32)).astype(BF)
+            sf[...] = zr[k - 1, 1].astype(F32) + zr[k - 1, 0].astype(F32)
 
         @pl.when(s == 0)
         def _():
-            sz[k - 1] = (zr[k - 1, 1].astype(F32) + value(slot_at(k, 1, 0))).astype(BF)
-
+            sf[...] = zr[k - 1, 1].astype(F32) + value(slot_at(k, 1, 0))
+
+        if k == 2:
+            sz[k - 1] = sf[...].astype(BF)
+            for h, d in ((0, 3), (1, 1)):
+                rows = pl.ds(h * QUARTER, QUARTER)
+                put(lambda rows=rows: sz.at[1, rows], lambda h=h: o2.at[h], lambda h=h: o2_r.at[h], at(dz=d))
+            return
+        h = k // 2
+        rows = pl.ds(h * QUARTER, QUARTER)
+        got(lambda: o2.at[h], lambda: o2_r.at[h])
+        sf[rows] += o2[h].astype(F32)
+        sz[k - 1] = sf[...].astype(BF)
         put(lambda: sz.at[k - 1], lambda: o1.at[k], lambda: o1_r.at[k], at(dz=-k))
 
     def di_rows(d, half):
@@ -264,11 +301,15 @@
             total = term if total is None else total + term
         return total
 
-    def collect_x():
+    def got_column():
         for k in (1, 3, 2):
             got(lambda k=k: xr.at[k - 1], lambda k=k: xr_r.at[k - 1])
+
+    def collect_far():
         sx[1] = (column(1, 0) + value(slot_at(0, 0, 1))).astype(BF)
         put(lambda: sx.at[1], lambda: o0.at[1], lambda: o0_r.at[1], at(dx=-2))
+
+    def collect_near():
         for d in (1, 3):
             @pl.when(z > 0)
             def _():
@@ -280,22 +321,25 @@
         inner = jnp.sum(normed * upstream, axis=-1, keepdims=True)
         return (upstream - normed * inner) / norm
 
-    for d in (1, 3, 2):
-        send_image(d)
+    for d, h in ((1, 0), (3, 1), (1, 1), (3, 0)):
+        send_image(d, h)
     along_z_high(2)
     along_z_high(1)
     along_z_high(3)
-    for d in (1, 3):
-        put_slot(own_low, 16 + d // 2, at(dx=d), z > 0)
+    put_slot(own_low, 16, at(dx=1), z > 0)
+    put_slot(own_low, 17, at(dx=3), z > 0)
     put_slot(own_low, slot_at(0, 0, 1), at(dx=2))
     along_z_low(2)
     put_slot(own_high, slot_at(0, 1, 1), at(dx=2))
     along_z_low(3)
     relay_image(0)
     relay_x(3)
-    relay_z_near((3, 1, 2))
+    relay_z_near(1, (3, 1, 2))
+    relay_z_near(3, (3, 1, 2))
     relay_z_far((2, 1, 3))
     along_z_low(1)
+    forward_image(1)
+    forward_image(3)
     relay_image(1)
     relay_image(3)
     relay_x(2)
@@ -309,19 +353,22 @@
     early(3, False)
     got_chunk(2)
     early(2, False)
+    inbound = len(pending)
     got_image(2)
     late((2, 3), True)
-    send_chunk(2)
-    send_chunk(3)
+    send_chunk(2, "10x")
+    send_chunk(3, "10x")
     got_chunk(1)
     early(1, False)
     late((0, 1), False)
-    send_chunk(0)
-    send_chunk(1)
+    send_chunk(0, "10x")
+    send_chunk(1, "10x")
     swap_images()
     return_images()
     collect_z(2)
-    collect_x()
+    got_column()
+    collect_far()
+    collect_near()
     collect_z(1)
     collect_z(3)
 
@@ -338,19 +385,13 @@
         got(lambda d=d: o0.at[d - 1], lambda d=d: o0_r.at[d - 1], z > 0)
         lower = lower + jnp.where(z > 0, o0[d - 1].astype(F32), 0.0)
     upper = value(slot_at(0, 1, 0))
-    for k in (0, 1, 3, 2):
+    for k in (0, 1, 3):
         got(lambda k=k: o1.at[k], lambda k=k: o1_r.at[k])
         upper = upper + o1[k].astype(F32)
     grad_texts[0:HALF] = unnormalize(tnormed[0:HALF], tnorm[0:HALF], lower)
     grad_texts[HALF:] = unnormalize(tnormed[HALF:], tnorm[HALF:], upper)
 
-    for make, cond in pending:
-        if cond is None:
-            make().wait_send()
-        else:
-            @pl.when(cond)
-            def _():
-                make().wait_send()
+    drain(len(pending))
 
 
 def local(images, texts, logit_scale, bias):
@@ -385,9 +426,13 @@
             pltpu.VMEM((3, HALF, WIDTH), BF),
             pltpu.VMEM((4, ROWS, WIDTH), BF),
             pltpu.VMEM((3, ROWS, WIDTH), BF),
+            pltpu.VMEM((HALF, WIDTH), F32),
+            pltpu.VMEM((2, QUARTER, WIDTH), BF),
+            dma((2,)),
             dma((2,)),
             dma((64,)),
             dma((4, 2)),
+            dma((4,)),
             dma((21,)),
             dma((3,)),
             dma((3, 2)),

time: 58.7 us -> 57.1 us (0.973)
  Pallas kernels: 54.4 us -> 52.9 us
    pallas_call x1, Pallas kernels: 54.4 us -> 52.9 us  [local(): pl.pallas_call(kernel, out_shape=[pltpu.VMEM((ROWS, WIDTH), F32)] * 2, in...]
where the time goes in v3:
time: 57.1 us; the launch traced here: 56.5 us
  Pallas kernels  52.9 us (93%)
  between operations  1.93 us (3%)
  local copies, waits for them, and re-layouts  1.63 us (3%)
    pallas_call x1, Pallas kernels, local(): pl.pallas_call(kernel, out_shape=[pltpu.VMEM((ROWS, WIDTH), F32)] * 2, in...  52.9 us
    unnamed x2, local copies, waits for them, and re-layouts  1.63 us

profile of v3, /device:TPU:32, one launch (start us, length us, event | category | flops | bytes accessed | tf_op | source)
XLA Modules:
  0.0 56.5 jit_solution(4242301428853281991)
XLA Ops:
  1.9 52.9 %pair_grads.1 = (f32[128,1152]{1,0:T(8,128)S(1)}, f32[128,1152]{1,0:T(8,128)S(1)}) custom-call(f32[1]{0:T(128)S(6)} %copy.10.logit_scale, f32[1]{0:T(128)S(6)} %copy.11.bias, bf16[128,1152]{1,0:T(8,128)(2,1)} %images_hbm.1, bf16[128,1152]{1,0:T(8,128)(2,1)} %texts_hbm.1), custom_call_target="tpu_custom_call" | custom-call | tf_op jit(solution)/shard_map/pair_grads/pallas_call | solution.py:402
  54.9 0.8 %copy.8 = f32[128,1152]{1,0:T(8,128)} copy(f32[128,1152]{1,0:T(8,128)S(1)} %get-tuple-element.2) | data formatting | bytes 1179648
  55.7 0.8 %copy.9 = f32[128,1152]{1,0:T(8,128)} copy(f32[128,1152]{1,0:T(8,128)S(1)} %get-tuple-element.3) | data formatting | bytes 1179648

commit v4 on v3

--- a/solution.py
+++ b/solution.py
@@ -31,7 +31,7 @@
     inormed, tnormed, inorm, tnorm,
     im, tb, di, pt, pb,
     xr, zr, o0, o1, dr, dyr,
-    sx, sz, sd, sy, sf, o2,
+    sx, sz, sd, sy, sf, o2, de, dl,
     o2_r, moved, send, im_h, im_r, tb_r, xr_r, zr_r, o0_r, o1_r, dr_r, dy_r,
 ):
     loop = lax.axis_index("loop")
@@ -211,6 +211,34 @@
         else:
             di[0:EARLY] += term
 
+    def early_images(k):
+        rows = pl.ds(CHUNK_AT[k] * 4 * HALF, 4 * HALF)
+        t = tb[rows]
+        i = im[0:3].reshape(EARLY, WIDTH)
+        logits = scale * lax.dot_general(t, i, (((1,), (1,)), ((), ())), preferred_element_type=F32) + shift
+        slopes = (1.0 / (1.0 + jnp.exp(-logits))).astype(BF)
+        de[...] = slopes
+        di[0:EARLY] += lax.dot_general(slopes, t, (((0,), (0,)), ((), ())), preferred_element_type=F32)
+
+    def early_texts(k):
+        rows = pl.ds(CHUNK_AT[k] * 4 * HALF, 4 * HALF)
+        pt[rows] = jnp.dot(de[...], im[0:3].reshape(EARLY, WIDTH), preferred_element_type=F32)
+
+    def late_images(ks):
+        rows = pl.ds(CHUNK_AT[ks[0]] * 4 * HALF, 4 * HALF * len(ks))
+        t = tb[rows]
+        i = im[3].reshape(2 * ROWS, WIDTH)
+        logits = scale * lax.dot_general(i, t, (((1,), (1,)), ((), ())), preferred_element_type=F32) + shift
+        slopes = (1.0 / (1.0 + jnp.exp(-logits))).astype(BF)
+        dl[...] = slopes
+        di[EARLY:] += jnp.dot(slopes, t, preferred_element_type=F32)
+
+    def late_texts(ks):
+        rows = pl.ds(CHUNK_AT[ks[0]] * 4 * HALF, 4 * HALF * len(ks))
+        i = im[3].reshape(2 * ROWS, WIDTH)
+        term = lax.dot_general(dl[...], i, (((0,), (0,)), ((), ())), preferred_element_type=F32)
+        pb[rows] = (pt[rows] + term).astype(BF)
+
     def late(ks, first):
         rows = pl.ds(CHUNK_AT[ks[0]] * 4 * HALF, 4 * HALF * len(ks))
         t = tb[rows]
@@ -218,7 +246,7 @@
         logits = scale * lax.dot_general(i, t, (((1,), (1,)), ((), ())), preferred_element_type=F32) + shift
         slopes = (1.0 / (1.0 + jnp.exp(-logits))).astype(BF)
         term = lax.dot_general(slopes, i, (((0,), (0,)), ((), ())), preferred_element_type=F32)
-        pb[rows] = (scale * (pt[rows] + term)).astype(BF)
+        pb[rows] = (pt[rows] + term).astype(BF)
         term = jnp.dot(slopes, t, preferred_element_type=F32)
         if first:
             di[EARLY:] = term
@@ -279,14 +307,17 @@
     def di_rows(d, half):
         return pl.ds(pl.multiple_of(IMAGE_AT[d] * 2 * ROWS + half * ROWS, ROWS), ROWS)
 
-    def swap_images():
-        for d in (2, 1, 3, 0):
-            sd[d] = (scale * di[di_rows(d, 1 - core)]).astype(BF)
-            put(lambda d=d: sd.at[d], lambda d=d: dr.at[d], lambda d=d: dr_r.at[d], at(dc=1))
+    def swap_image(d):
+        sd[d] = di[di_rows(d, 1 - core)].astype(BF)
+        put(lambda: sd.at[d], lambda: dr.at[d], lambda: dr_r.at[d], at(dc=1))
+
+    def return_image(d):
+        sy[d - 1] = mine(d).astype(BF)
+        put(lambda: sy.at[d - 1], lambda: dyr.at[d - 1], lambda: dy_r.at[d - 1], at(dy=-d))
 
     def mine(d):
         got(lambda: dr.at[d], lambda: dr_r.at[d])
-        return scale * di[di_rows(d, core)] + dr[d].astype(F32)
+        return di[di_rows(d, core)] + dr[d].astype(F32)
 
     def return_images():
         for d in (2, 1, 3):
@@ -359,11 +390,15 @@
     send_chunk(2, "10x")
     send_chunk(3, "10x")
     got_chunk(1)
-    early(1, False)
-    late((0, 1), False)
+    late_images((0, 1))
+    swap_image(2)
+    early_images(1)
+    for d in (1, 3, 0):
+        swap_image(d)
+    early_texts(1)
+    late_texts((0, 1))
     send_chunk(0, "10x")
     send_chunk(1, "10x")
-    swap_images()
     return_images()
     collect_z(2)
     got_column()
@@ -399,7 +434,7 @@
     vmem = pl.BlockSpec(memory_space=pltpu.VMEM)
     smem = pl.BlockSpec(memory_space=pltpu.SMEM)
     dma = pltpu.SemaphoreType.DMA
-    return pl.pallas_call(
+    grads = pl.pallas_call(
         kernel,
         out_shape=[pltpu.VMEM((ROWS, WIDTH), F32)] * 2,
         in_specs=[smem, smem, hbm, hbm],
@@ -428,6 +463,8 @@
             pltpu.VMEM((3, ROWS, WIDTH), BF),
             pltpu.VMEM((HALF, WIDTH), F32),
             pltpu.VMEM((2, QUARTER, WIDTH), BF),
+            pltpu.VMEM((4 * HALF, EARLY), BF),
+            pltpu.VMEM((2 * ROWS, 8 * HALF), BF),
             dma((2,)),
             dma((2,)),
             dma((64,)),
@@ -446,6 +483,7 @@
         ),
         name="pair_grads",
     )(logit_scale, bias, images, texts)
+    return tuple(logit_scale[0] * grad for grad in grads)
 
 
 def solution(mesh):

time: 57.1 us -> 56.3 us (0.986)
  local copies, waits for them, and re-layouts: 1.63 us -> 0 us
  other arithmetic: 0 us -> 1.09 us
    unnamed x2 -> x0, local copies, waits for them, and re-layouts: 1.63 us -> none
    mul x0 -> x1, other arithmetic: none -> 1.09 us  [local(): return tuple((logit_scale[0] * grad for grad in grads))]
where the time goes in v4:
time: 56.3 us; the launch traced here: 56.2 us
  Pallas kernels  53.2 us (94%)
  between operations  1.93 us (3%)
  other arithmetic  1.09 us (2%)
    pallas_call x1, Pallas kernels, local(): pl.pallas_call(kernel, out_shape=[pltpu.VMEM((ROWS, WIDTH), F32)] * 2, in...  53.2 us

profile of v4, /device:TPU:32, one launch (start us, length us, event | category | flops | bytes accessed | tf_op | source)
XLA Modules:
  0.0 56.2 jit_solution(2547616668088514619)
XLA Ops:
  1.9 53.2 %pair_grads.1 = (f32[128,1152]{1,0:T(8,128)S(1)}, f32[128,1152]{1,0:T(8,128)S(1)}) custom-call(f32[1]{0:T(128)} %copy.6.logit_scale, f32[1]{0:T(128)S(6)} %copy.7.bias, bf16[128,1152]{1,0:T(8,128)(2,1)} %images_hbm.1, bf16[128,1152]{1,0:T(8,128)(2,1)} %texts_hbm.1), custom_call_target="tpu_custom_call" | custom-call | tf_op jit(solution)/shard_map/pair_grads/pallas_call | solution.py:437
  55.1 1.1 %broadcast_multiply_fusion = (f32[128,1152]{1,0:T(8,128)}, f32[128,1152]{1,0:T(8,128)}) fusion(f32[128,1152]{1,0:T(8,128)S(1)} %get-tuple-element.5, f32[]{:T(128)} %bitcast.1, f32[128,1152]{1,0:T(8,128)S(1)} %get-tuple-element.4), kind=kLoop, calls=%fused_computation | loop fusion | flops 294912 | bytes 2359300 | tf_op jit(solution)/shard_map/mul | solution.py:486

commit v5 on v4

--- a/solution.py
+++ b/solution.py
@@ -31,8 +31,8 @@
     inormed, tnormed, inorm, tnorm,
     im, tb, di, pt, pb,
     xr, zr, o0, o1, dr, dyr,
-    sx, sz, sd, sy, sf, o2, de, dl,
-    o2_r, moved, send, im_h, im_r, tb_r, xr_r, zr_r, o0_r, o1_r, dr_r, dy_r,
+    sx, sz, sd, sy, sf, o2, de, dl, y2, sm,
+    o2_r, y2_r, moved, send, im_h, im_r, tb_r, xr_r, zr_r, o0_r, o1_r, dr_r, dy_r,
 ):
     loop = lax.axis_index("loop")
     group = lax.axis_index("group")
@@ -311,18 +311,32 @@
         sd[d] = di[di_rows(d, 1 - core)].astype(BF)
         put(lambda: sd.at[d], lambda: dr.at[d], lambda: dr_r.at[d], at(dc=1))
 
-    def return_image(d):
-        sy[d - 1] = mine(d).astype(BF)
-        put(lambda: sy.at[d - 1], lambda: dyr.at[d - 1], lambda: dy_r.at[d - 1], at(dy=-d))
-
     def mine(d):
         got(lambda: dr.at[d], lambda: dr_r.at[d])
         return di[di_rows(d, core)] + dr[d].astype(F32)
 
+    def put_image(d, h):
+        rows = pl.ds(h * HALF, HALF)
+        put(lambda: sy.at[d - 1, rows], lambda: dyr.at[d // 2, rows], lambda: dy_r.at[d // 2, h], at(dy=-d))
+
     def return_images():
-        for d in (2, 1, 3):
-            sy[d - 1] = mine(d).astype(BF)
-            put(lambda d=d: sy.at[d - 1], lambda d=d: dyr.at[d - 1], lambda d=d: dy_r.at[d - 1], at(dy=-d))
+        sy[1] = mine(2).astype(BF)
+        for h, d in ((0, 3), (1, 1)):
+            rows = pl.ds(h * HALF, HALF)
+            put(lambda rows=rows: sy.at[1, rows], lambda h=h: y2.at[h], lambda h=h: y2_r.at[h], at(dy=d))
+        for d in (1, 3):
+            sm[d // 2] = mine(d)
+            h = 1 - d // 2
+            sy[d - 1, pl.ds(h * HALF, HALF)] = sm[d // 2, pl.ds(h * HALF, HALF)].astype(BF)
+            put_image(d, h)
+
+    def return_sums():
+        for d in (1, 3):
+            h = d // 2
+            rows = pl.ds(h * HALF, HALF)
+            got(lambda: y2.at[h], lambda: y2_r.at[h])
+            sy[d - 1, rows] = (sm[h, rows] + y2[h].astype(F32)).astype(BF)
+            put_image(d, h)
 
     def column(j, wrap):
         total = None
@@ -352,11 +366,11 @@
         inner = jnp.sum(normed * upstream, axis=-1, keepdims=True)
         return (upstream - normed * inner) / norm
 
-    for d, h in ((1, 0), (3, 1), (1, 1), (3, 0)):
-        send_image(d, h)
     along_z_high(2)
     along_z_high(1)
     along_z_high(3)
+    for d, h in ((1, 0), (3, 1), (1, 1), (3, 0)):
+        send_image(d, h)
     put_slot(own_low, 16, at(dx=1), z > 0)
     put_slot(own_low, 17, at(dx=3), z > 0)
     put_slot(own_low, slot_at(0, 0, 1), at(dx=2))
@@ -384,10 +398,10 @@
     early(3, False)
     got_chunk(2)
     early(2, False)
-    inbound = len(pending)
     got_image(2)
-    late((2, 3), True)
+    late((2,), True)
     send_chunk(2, "10x")
+    late((3,), False)
     send_chunk(3, "10x")
     got_chunk(1)
     late_images((0, 1))
@@ -401,6 +415,7 @@
     send_chunk(1, "10x")
     return_images()
     collect_z(2)
+    return_sums()
     got_column()
     collect_far()
     collect_near()
@@ -408,9 +423,11 @@
     collect_z(3)
 
     total = mine(0)
-    for d in (1, 3, 2):
-        got(lambda d=d: dyr.at[d - 1], lambda d=d: dy_r.at[d - 1])
-        total = total + dyr[d - 1].astype(F32)
+    for d in (1, 3):
+        for h in (0, 1):
+            rows = pl.ds(h * HALF, HALF)
+            got(lambda: dyr.at[d // 2, rows], lambda: dy_r.at[d // 2, h])
+        total = total + dyr[d // 2].astype(F32)
     grad_images[...] = unnormalize(inormed[...], inorm[...], total)
 
     lower = column(0, 0) + value(slot_at(0, 0, 0))
@@ -465,6 +482,9 @@
             pltpu.VMEM((2, QUARTER, WIDTH), BF),
             pltpu.VMEM((4 * HALF, EARLY), BF),
             pltpu.VMEM((2 * ROWS, 8 * HALF), BF),
+            pltpu.VMEM((2, HALF, WIDTH), BF),
+            pltpu.VMEM((2, ROWS, WIDTH), F32),
+            dma((2,)),
             dma((2,)),
             dma((2,)),
             dma((64,)),
@@ -476,7 +496,7 @@
             dma((3,)),
             dma((4,)),
             dma((4,)),
-            dma((3,)),
+            dma((2, 2)),
         ],
         compiler_params=pltpu.CompilerParams(
             collective_id=0, has_side_effects=True, vmem_limit_bytes=56 * 2**20

time: 56.3 us -> 55.5 us (0.986)
  Pallas kernels: 53.2 us -> 52.3 us
    pallas_call x1, Pallas kernels: 53.2 us -> 52.3 us  [local(): pl.pallas_call(kernel, out_shape=[pltpu.VMEM((ROWS, WIDTH), F32)] * 2, in...]
where the time goes in v5:
time: 55.5 us; the launch traced here: 55.4 us
  Pallas kernels  52.3 us (94%)
  between operations  1.93 us (3%)
  other arithmetic  1.09 us (2%)
    pallas_call x1, Pallas kernels, local(): pl.pallas_call(kernel, out_shape=[pltpu.VMEM((ROWS, WIDTH), F32)] * 2, in...  52.3 us

profile of v5, /device:TPU:32, one launch (start us, length us, event | category | flops | bytes accessed | tf_op | source)
XLA Modules:
  0.0 55.4 jit_solution(4634572389938214949)
XLA Ops:
  1.9 52.3 %pair_grads.1 = (f32[128,1152]{1,0:T(8,128)S(1)}, f32[128,1152]{1,0:T(8,128)S(1)}) custom-call(f32[1]{0:T(128)} %copy.6.logit_scale, f32[1]{0:T(128)S(6)} %copy.7.bias, bf16[128,1152]{1,0:T(8,128)(2,1)} %images_hbm.1, bf16[128,1152]{1,0:T(8,128)(2,1)} %texts_hbm.1), custom_call_target="tpu_custom_call" | custom-call | tf_op jit(solution)/shard_map/pair_grads/pallas_call | solution.py:454
  54.3 1.1 %broadcast_multiply_fusion = (f32[128,1152]{1,0:T(8,128)}, f32[128,1152]{1,0:T(8,128)}) fusion(f32[128,1152]{1,0:T(8,128)S(1)} %get-tuple-element.5, f32[]{:T(128)} %bitcast.1, f32[128,1152]{1,0:T(8,128)S(1)} %get-tuple-element.4), kind=kLoop, calls=%fused_computation | loop fusion | flops 294912 | bytes 2359300 | tf_op jit(solution)/shard_map/mul | solution.py:506
